TPU v7x, 512 devices: a whole 4x8x8 slice. The times are simulated.
512 devices in a mesh: kv: 4 (over z_lo), blk: 128 (over z_hi, x, y, core).
Axes of the slice: x: 4, y: 8, z: 8 (z_hi: 2, z_lo: 4; z = z_hi * 4 + z_lo), core: 2. Of those that a mesh axis runs over, the one named last changes fastest.
Arguments:
- queries: bfloat16 [10240, 2048], P('blk', 'kv'), may hold values from -32 to 32, as said below
- keys: bfloat16 [10240, 512], P('blk', 'kv'), may hold values from -7 to 7, as said below
- values: bfloat16 [10240, 512], P('blk', 'kv'), may hold values from -6 to 6
- lengths: int32 [64], replicated, may hold values from 1 to 80, 2048 in all
- out_weight: bfloat16 [4096, 2048], P('blk', 'kv'), may hold values from -0.125 to 0.125
Outputs:
- hidden: bfloat16 [10240, 4096], P('blk', 'kv')
- cache_keys: bfloat16 [10240, 512], P('blk', 'kv')
Inputs may be any that keep to these rules, and one draw needn't show every extreme that they name: `queries`: rotary inputs of order one; in some rows a query head may be a multiple of its key head. `keys`: key projections of order one. `lengths`: each short prompt is 1 to 80 tokens long, one of them exactly 80; their sum is 2048.
All inputs are finite; a program needn't handle non-finite values.
Results may differ from a plain program's by a relative error of at most 0.0095.
Values may be sent and summed in bfloat16 or wider, within the bound.
A program may use at most 64 MiB of HBM per device.

v0:
```python
import jax
import jax.numpy as jnp
from jax import lax
from jax.sharding import PartitionSpec as P

rope_base = 500000.0


def locate(index, starts):
    hit = starts[None, :] <= index[:, None]
    segment = jnp.sum(hit.astype(jnp.int32), axis=1) - 1
    offset = jnp.max(jnp.where(hit, starts[None, :], 0), axis=1)
    return (segment, offset)


def rotate(field, positions):
    half = field.shape[-1] // 2
    steps = jnp.arange(half).astype(jnp.float32) * (2.0 / field.shape[-1])
    inverse = jnp.power(jnp.float32(rope_base), -steps)
    angle = positions.astype(jnp.float32)[:, None, None] * inverse[None, None, :]
    cosine = jnp.cos(angle)
    sine = jnp.sin(angle)
    first = field[..., :half].astype(jnp.float32)
    second = field[..., half:].astype(jnp.float32)
    return jnp.concatenate(
        [first * cosine - second * sine, second * cosine + first * sine], axis=-1
    )


def body(queries, keys, values, lengths, out_weight):
    tok_rows = queries.shape[0]
    head_size = keys.shape[1]
    groups = queries.shape[1] // head_size
    total_len = tok_rows * lax.axis_size("blk")
    long_len = total_len - jnp.sum(lengths)
    shifted = jnp.concatenate([jnp.zeros((1,), jnp.int32), jnp.cumsum(lengths)[:-1]])
    starts = jnp.concatenate([jnp.zeros((1,), jnp.int32), long_len + shifted])
    first_tok = lax.axis_index("blk") * tok_rows
    query_idx = first_tok + jnp.arange(tok_rows)
    query_seg, query_off = locate(query_idx, starts)
    positions = query_idx - query_off
    rot_keys = (
        rotate(keys.reshape(tok_rows, 1, head_size), positions)
        .astype(jnp.bfloat16)
        .reshape(tok_rows, head_size)
    )
    rot_queries = rotate(queries.reshape(tok_rows, groups, head_size), positions).astype(
        jnp.bfloat16
    )
    query_rows = jnp.transpose(rot_queries, (1, 0, 2)).reshape(groups * tok_rows, head_size)
    row_idx = jnp.tile(query_idx, groups)
    row_seg = jnp.tile(query_seg, groups)
    scale = 1.0 / head_size**0.5
    row_count = groups * tok_rows
    key_piece = lax.all_gather(rot_keys, "blk", axis=0, tiled=True)
    value_piece = lax.all_gather(values, "blk", axis=0, tiled=True)
    row_max = jnp.full((row_count,), -1e30, jnp.float32)
    span = key_piece.shape[0]
    key_idx = jnp.arange(span)
    key_seg, key_off = locate(key_idx, starts)
    live = (key_seg[None, :] == row_seg[:, None]) & (key_idx[None, :] <= row_idx[:, None])
    scores = (
        jnp.einsum("rd,nd->rn", query_rows, key_piece, preferred_element_type=jnp.float32) * scale
    )
    scores = jnp.where(live, scores, -1e30)
    new_max = jnp.maximum(row_max, jnp.max(scores, axis=1))
    probs = jnp.where(live, jnp.exp(scores - new_max[:, None]), 0.0)
    new_sum = jnp.sum(probs, axis=1)
    new_weighted = jnp.dot(
        probs.astype(jnp.bfloat16), value_piece, preferred_element_type=jnp.float32
    )
    attended = (new_weighted / new_sum[:, None]).astype(jnp.bfloat16)
    attended = jnp.transpose(attended.reshape(groups, tok_rows, head_size), (1, 0, 2)).reshape(
        tok_rows, groups * head_size
    )
    terms = jnp.einsum(
        "tk,nk->tn",
        attended,
        lax.all_gather(out_weight, "blk", axis=0, tiled=True),
        preferred_element_type=jnp.float32,
    )
    hidden = lax.psum_scatter(terms.astype(jnp.bfloat16), "kv", scatter_dimension=1, tiled=True)
    return (hidden, rot_keys)


def solution(mesh):
    return jax.shard_map(
        body,
        mesh=mesh,
        in_specs=(P("blk", "kv"), P("blk", "kv"), P("blk", "kv"), P(), P("blk", "kv")),
        out_specs=(P("blk", "kv"), P("blk", "kv")),
        check_vma=False,
    )
```

profile of v0, /device:TPU:6, one launch (start us, length us, event | category | flops | bytes accessed | tf_op | source)
XLA Modules:
  0.0 453.4 jit_solution(1033060220301884632)
XLA Ops:
  7.2 0.0 all-gather.4.cloned.1.call-start
  7.2 0.7 copy.13
  8.0 1.3 reduce_sum.36
  9.3 0.1 reduce-window.4
  9.4 0.1 slice_reduce_fusion
  10.1 0.1 add_add_fusion
  10.2 0.1 pad_add_fusion
  10.3 0.1 fusion.26
  10.4 1.0 fusion.29
  11.4 0.7 pad_maximum_fusion
  12.1 0.0 all-gather.4.cloned.1.call-update
  12.2 0.0 all-gather.6.cloned.1.call-start
  12.2 0.7 all-gather.6.cloned.1.call-update
  12.9 0.0 all-gather.8.cloned.1.call-start
  13.0 0.7 all-gather.8.cloned.1.call-update
  13.6 0.0 reduce-scatter.2.cloned.1.call-start
  13.7 0.9 reshape.179
  14.6 0.2 multiply_cosine_fusion.1
  14.8 0.2 fusion.13
  15.0 0.1 maximum_bitcast_fusion
  15.2 0.1 eq.16
  15.3 0.1 le.48
  15.4 0.5 convert_reduce_fusion
  15.8 134.9 %all-gather.4.cloned.1.call-done = bf16[10240,128]{1,0:T(8,128)(2,1)} async-done(((bf16[80,128]{1,0:T(8,128)(2,1)}), bf16[10240,128]{1,0:T(8,128)(2,1)}) %all-gather.4.cloned.1.call-update) | async-done | bytes 2621456 | tf_op jit(solution)/shard_map/all_gather | solution.py:55
  150.8 5.8 %fusion.31 = (f32[320]{0:T(512)S(1)}, f32[320,10240]{1,0:T(8,128)S(1)}) fusion(bf16[320,128]{1,0:T(8,128)(2,1)S(1)} %bitcast.20, bf16[10240,128]{1,0:T(8,128)(2,1)} %all-gather.4.cloned.1.call-done, s32[320]{0:T(512)S(1)} %le.48, s32[320]{0:T(512)S(1)} %eq.16, s32[10240]{0:T(1024)S(1)} %broadcast_add_fusion), kind=kOutput, calls=%fused_computation.53 | convolution fusion | flops 858521280 | bytes 15855360 | tf_op jit(solution)/shard_map/rd,nd->rn/dot_general | solution.py:63
  156.6 0.0 copy-start
  156.6 4.6 %copy-done = f32[320,10240]{1,0:T(8,128)} copy-done((f32[320,10240]{1,0:T(8,128)}, f32[320,10240]{1,0:T(8,128)S(1)}, u32[]{:S(2)}) %copy-start) | copy-done | bytes 13107224
  161.2 4.4 fusion.2
  165.6 115.6 %all-gather.6.cloned.1.call-done = bf16[10240,128]{1,0:T(8,128)(2,1)} async-done(((bf16[80,128]{1,0:T(8,128)(2,1)}), bf16[10240,128]{1,0:T(8,128)(2,1)}) %all-gather.6.cloned.1.call-update) | async-done | bytes 2621456 | tf_op jit(solution)/shard_map/all_gather | solution.py:56
  281.2 8.8 %fusion.9 = bf16[320,128]{1,0:T(8,128)(2,1)S(1)} fusion(bf16[10240,128]{1,0:T(8,128)(2,1)} %all-gather.6.cloned.1.call-done, f32[320,10240]{1,0:T(8,128)} %copy-done, f32[320]{0:T(512)S(1)} %broadcast_maximum_fusion, s32[320]{0:T(512)S(1)} %le.48, s32[10240]{0:T(1024)S(1)} %broadcast_add_fusion, s32[320]{0:T(512)S(1)} %eq.16, f32[320]{0:T(512)S(1)} %fusion.2), kind=kOutput, calls=%fused_computation.12 | convolution fusion | flops 858603520 | bytes 15856640 | tf_op jit(solution)/shard_map/dot_general | solution.py:69
  290.1 128.4 %all-gather.8.cloned.1.call-done = bf16[4096,512]{1,0:T(8,128)(2,1)} async-done(((bf16[32,512]{1,0:T(8,128)(2,1)}), bf16[4096,512]{1,0:T(8,128)(2,1)}) %all-gather.8.cloned.1.call-update) | async-done | bytes 4194320 | tf_op jit(solution)/shard_map/all_gather | solution.py:79
  418.5 4.4 convolution_convert_fusion
  422.9 0.0 reduce-scatter.2.cloned.1.call-update
  422.9 23.9 %reduce-scatter.2.cloned.1.call-done = bf16[80,1024]{1,0:T(8,128)(2,1)} async-done(((bf16[80,4096]{1,0:T(8,128)(2,1)}), bf16[80,1024]{1,0:T(8,128)(2,1)}) %reduce-scatter.2.cloned.1.call-update) | async-done | bytes 163856 | tf_op jit(solution)/shard_map/reduce_scatter | solution.py:82
  (9 shorter events, 0.1 us)
Async XLA Ops:
  7.2 143.6 %all-gather.4.cloned.1.call-start = ((), (), s32[]{:S(2)}) async-start(), calls=%async_computation.1 | async-start | bytes 2641920 | tf_op jit(solution)/shard_map/all_gather | solution.py:55
  12.2 269.0 %all-gather.6.cloned.1.call-start = ((), (), s32[]{:S(2)}) async-start(), calls=%async_computation.2 | async-start | bytes 2641920 | tf_op jit(solution)/shard_map/all_gather | solution.py:56
  12.9 405.6 %all-gather.8.cloned.1.call-start = ((), (), s32[]{:S(2)}) async-start(), calls=%async_computation.3 | async-start | bytes 4227072 | tf_op jit(solution)/shard_map/all_gather | solution.py:79
  13.6 433.2 %reduce-scatter.2.cloned.1.call-start = ((), (), s32[]{:S(2)}) async-start(), calls=%async_computation.4 | async-start | bytes 819200 | tf_op jit(solution)/shard_map/reduce_scatter | solution.py:82
  156.6 4.7 %copy-start = (f32[320,10240]{1,0:T(8,128)}, f32[320,10240]{1,0:T(8,128)S(1)}, u32[]{:S(2)}) copy-start(f32[320,10240]{1,0:T(8,128)S(1)} %get-tuple-element.11) | copy-start | bytes 39321604
Sparse Core Ops, SparseCore 0:
  13.0 137.6 all-gather.3
  155.2 125.9 all-gather.5
  285.8 132.6 all-gather.7
  423.0 23.7 reduce-scatter.1
where the time goes:
time: 454 us; the launch traced here: 453 us
  waiting for transfers between devices  404 us (89%)
  matrix products  19 us (4%)
  between operations  14.5 us (3%)
  other arithmetic  8.74 us (2%)
  local copies, waits for them, and re-layouts  6.64 us (1%)
    all_gather x1, waiting for transfers between devices, body(): key_piece = lax.all_gather(rot_keys, 'blk', axis=0, tiled=True)  135 us
    all_gather x1, waiting for transfers between devices, body(): lax.all_gather(out_weight, 'blk', axis=0, tiled=True)  128 us
    all_gather x1, waiting for transfers between devices, body(): value_piece = lax.all_gather(values, 'blk', axis=0, tiled=True)  116 us
    reduce_scatter x1, waiting for transfers between devices, body(): lax.psum_scatter(terms.astype(jnp.bfloat16), 'kv', scatter_dimension=1, t...  23.9 us
  transfers between devices with their start and end apart: 4, of which 4 were waited for; matrix products, arithmetic and copies ran while one was open for 5% of the time, Pallas kernels for 0%

commit v1 on v0

v1 whole, which is shorter than its diff:
```python
import functools

import jax
import jax.numpy as jnp
import numpy as np
from jax import lax
from jax.experimental import pallas as pl
from jax.experimental.pallas import tpu as pltpu
from jax.sharding import PartitionSpec as P

MESH = pl.DeviceIdType.MESH
T, HD, H, NX, NY, G = 80, 128, 4, 4, 8, 4
R = H * T
SUP = 16 * T
CH = NY * T
LONG_BLOCKS = 102
LONG_TOKENS = 8192
TOKENS = 10240
NEG = -1e30
SCALE = float(np.log2(np.e) / np.sqrt(HD))


def dot_nt(a, b):
    return lax.dot_general(a, b, (((1,), (1,)), ((), ())), preferred_element_type=jnp.float32)


def kernel(
    q_ref, k_ref, v_ref, len_ref, w_ref, inv_ref, out_ref, cache_ref,
    kv, qb, acc, mx, sm, osend, ssend, obuf, sbuf, ab, wb, col,
    ys, yr, zs, zr, fs, fr, cs, cr, qs, qr, os_, or_, ss, sr, as_, ar, wds, wdr, wrs, wrr, wcs, wcr, lsem,
):
    blk, g = lax.axis_index("blk"), lax.axis_index("kv")
    c = lax.rem(blk, 2)
    y = lax.rem(lax.div(blk, 2), NY)
    x = lax.rem(lax.div(blk, 16), NX)
    zh = lax.div(blk, 64)
    dest_g = 2 * zh + lax.div(x, 2)
    half = lax.rem(x, 2)

    def at(zh_=zh, x_=x, y_=y, c_=c, g_=g):
        return {"blk": ((zh_ * NX + x_) * NY + y_) * 2 + c_, "kv": g_}

    def send(src, dst, s, r, dev):
        return pltpu.make_async_remote_copy(
            src_ref=src, dst_ref=dst, send_sem=s, recv_sem=r, device_id=dev, device_id_type=MESH
        )

    def yp(d):
        return lax.rem(y + d + NY, NY)

    def xp(d):
        return lax.rem(x + d, NX)

    def gp(d):
        return lax.rem(g + d, G)

    bar = pltpu.get_barrier_semaphore()

    def hello(dev):
        pl.semaphore_signal(bar, inc=1, device_id=dev, device_id_type=MESH)

    hello(at(zh_=1 - zh))
    hello(at(c_=1 - c))
    for d in range(1, NY):
        hello(at(y_=yp(d)))
    for d in range(1, NX):
        hello(at(x_=xp(d)))
    for d in range(1, G):
        hello(at(g_=gp(d)))
    src_zh, src_x = lax.div(g, 2), 2 * lax.rem(g, 2)
    is_src = (src_zh == zh) & (lax.div(x, 2) == lax.rem(g, 2))
    for a in range(2):
        for d in range(G):
            if d == 0:
                @pl.when(jnp.logical_not(is_src & (half == a)))
                def _(a=a):
                    hello(at(zh_=src_zh, x_=src_x + a))
            else:
                hello(at(zh_=src_zh, x_=src_x + a, g_=gp(d)))

    lens = jnp.broadcast_to(len_ref[...].astype(jnp.float32), (8, 64))
    tri = (lax.broadcasted_iota(jnp.int32, (64, 64), 0) < lax.broadcasted_iota(jnp.int32, (64, 64), 1))
    before = jnp.dot(lens, tri.astype(jnp.float32), preferred_element_type=jnp.float32)[:1]
    starts = before + (TOKENS - jnp.sum(lens[:1], axis=1, keepdims=True))

    def first_of(tok):
        return jnp.max(jnp.where(starts <= tok, starts, 0.0), axis=1, keepdims=True)

    row = lax.broadcasted_iota(jnp.int32, (T, 1), 0)
    tok = (row + blk * T).astype(jnp.float32)
    angle = (tok - first_of(tok)) * inv_ref[...]
    cosine = jnp.cos(angle)
    lane = lax.broadcasted_iota(jnp.int32, (T, HD), 1)
    sine = jnp.where(lane < HD // 2, -1.0, 1.0) * jnp.sin(angle)

    def rotate(f):
        f = f.astype(jnp.float32)
        return (f * cosine + pltpu.roll(f, HD // 2, 1) * sine).astype(jnp.bfloat16)

    rk = rotate(k_ref[...])
    cache_ref[...] = rk
    kv[zh, c, y, 0] = rk
    kv[zh, c, y, 1] = v_ref[...]
    for h in range(H):
        qb[x, h * T:(h + 1) * T, :] = rotate(q_ref[:, h * HD:(h + 1) * HD])

    pl.semaphore_wait(bar, 2 + (NY - 1) + (NX - 1) + (G - 1) + 7 + jnp.where(dest_g == g, 0, 1))

    mine = kv.at[zh, c, y]
    zsend = send(mine, mine, zs, zr, at(zh_=1 - zh))

    @pl.when(zh == 0)
    def _():
        zsend.start()

    ysend = [send(mine, mine, ys.at[d - 1], yr.at[d - 1], at(y_=yp(d))) for d in range(1, NY)]
    qsend = [send(qb.at[x], qb.at[x], qs.at[d - 1], qr.at[d - 1], at(x_=xp(d))) for d in range(1, NX)]
    for d in (4, 3, 5, 2, 6, 1, 7):
        ysend[d - 1].start()
    for s in qsend:
        s.start()
    slot = wb.at[y, c, g, half]
    wsend = []
    for dz in range(2):
        for dx in range(NX):
            i = dz * NX + dx
            s = send(w_ref, slot, wds.at[i], wdr.at[half, g], at(zh_=lax.rem(zh + dz, 2), x_=xp(dx), g_=dest_g))
            if i:
                s.start()
            else:
                @pl.when(dest_g != g)
                def _(s=s):
                    s.start()
            wsend.append(s)
    own_w = pltpu.make_async_copy(w_ref, slot, lsem)

    @pl.when(dest_g == g)
    def _():
        own_w.start()

    for i in range(NX):
        tk = (row + ((zh * NX + i) * 16 + 2 * y + c) * T).astype(jnp.float32)
        st = first_of(tk)
        both = jnp.where(lax.broadcasted_iota(jnp.int32, (T, HD), 1) == 0, tk, st)
        for h in range(H):
            col[i, h * T:(h + 1) * T, :] = both
    mx[...] = jnp.full(mx.shape, NEG, jnp.float32)
    sm[...] = jnp.zeros(sm.shape, jnp.float32)
    acc[...] = jnp.zeros(acc.shape, jnp.float32)

    other = kv.at[0, c, y]
    fsend = [send(other, other, fs.at[d - 1], fr.at[d - 1], at(y_=yp(d))) for d in range(1, NY)]

    @pl.when(zh == 1)
    def _():
        zsend.wait_recv()
        for d in (4, 3, 5, 2, 6, 1, 7):
            fsend[d - 1].start()

    def chunk(zk, ck):
        sk = zk * NX + x
        r = lax.broadcasted_iota(jnp.int32, (1, CH), 1)
        key_tok = ((r + lax.div(r, T) * T) + sk * SUP + ck * T).astype(jnp.float32)

        def one(i, _):
            sq = zh * NX + i
            b = sq * 16 + 2 * y + c
            near = (sk == sq) | ((sk == sq - 1) & (2 * y + c == 0))
            live = (sk <= sq) & ((b <= LONG_BLOCKS) | near)
            edge = (sk == sq) | (b >= LONG_BLOCKS)

            def work(masked):
                keys = kv[zk, ck, :, 0].reshape(CH, HD)
                vals = kv[zk, ck, :, 1].reshape(CH, HD)
                s = dot_nt(qb[i], keys) * SCALE
                if masked:
                    ok = (key_tok <= col[i, :, 0:1]) & (key_tok >= col[i, :, 1:2])
                    s = jnp.where(ok, s, NEG)
                old = mx[i, :, 0:1]
                new = jnp.maximum(old, jnp.max(s, axis=1, keepdims=True))
                p = jnp.exp2(s - new)
                if masked:
                    p = jnp.where(ok, p, 0.0)
                keep = jnp.exp2(old - new)
                sm[i] = jnp.broadcast_to(sm[i, :, 0:1] * keep + jnp.sum(p, axis=1, keepdims=True), (R, HD))
                mx[i] = jnp.broadcast_to(new, (R, HD))
                acc[i] = acc[i] * keep + jnp.dot(p.astype(jnp.bfloat16), vals, preferred_element_type=jnp.float32)

            @pl.when(live & edge)
            def _():
                work(True)

            @pl.when(live & jnp.logical_not(edge))
            def _():
                work(False)

            return 0

        lax.fori_loop(0, NX, one, 0)

    def over(zk, i):
        return send(kv.at[zk, c], kv.at[zk, c], cs.at[i], cr.at[i], at(c_=1 - c))

    near_half = over(zh, 0)
    far_half = over(0, 1)
    for s in ysend:
        s.wait_recv()
    near_half.start()
    for s in qsend:
        s.wait_recv()
    chunk(zh, c)

    def ring(sign, step, p):
        i = 0 if sign > 0 else 1
        piece = wb.at[yp(-sign * (step - 1)), c, pl.ds(2 * p, 2)]
        return send(piece, piece, wrs.at[i, step - 1, p], wrr.at[i, step - 1, p], at(y_=yp(sign)))

    def ring_pieces(sign, step):
        return (0, 1) if step < 4 else ((0,) if sign > 0 else (1,))

    def w_over(yy, i):
        return send(wb.at[yy, c], wb.at[yy, c], wcs.at[i], wcr.at[i], at(c_=1 - c))

    all_ring = [(sign, step, p) for step in range(1, 5) for sign in (1, -1) for p in ring_pieces(sign, step)]

    def w_begin():
        for a in range(2):
            for gg in range(G):
                is_own = (gg == g) & (dest_g == g) & (half == a)

                @pl.when(is_own)
                def _():
                    own_w.wait()

                @pl.when(jnp.logical_not(is_own))
                def _(a=a, gg=gg):
                    send(w_ref, wb.at[y, c, gg, a], wds.at[0], wdr.at[a, gg], at(c_=1 - c)).wait_recv()
        for p in range(2):
            for sign in (1, -1):
                ring(sign, 1, p).start()
        w_over(y, 0).start()

    def w_step(step):
        for p in range(2):
            for sign in (1, -1):
                if p in ring_pieces(sign, step):
                    ring(sign, step, p).wait_recv()
                    if step < 4 and p in ring_pieces(sign, step + 1):
                        ring(sign, step + 1, p).start()
        w_over(yp(step), step).start()
        if step < 4:
            w_over(yp(-step), 8 - step).start()

    w_begin()
    near_half.wait_recv()
    chunk(zh, 1 - c)

    @pl.when(zh == 1)
    def _():
        for s in fsend:
            s.wait_recv()
        far_half.start()
        chunk(0, c)
        far_half.wait_recv()
        chunk(0, 1 - c)

    lane_r = lax.broadcasted_iota(jnp.int32, (R, HD), 1)

    def pack(d, _):
        i = lax.rem(x + d, NX)
        osend[i] = acc[i].astype(jnp.bfloat16)
        ssend[i] = jnp.transpose(jnp.where(lane_r == 0, mx[i], sm[i]))[:8]
        return 0

    lax.fori_loop(0, NX, pack, 0)
    ox = [send(osend.at[xp(d)], obuf.at[x], os_.at[d - 1], or_.at[d - 1], at(x_=xp(d))) for d in range(1, NX)]
    sx = [send(ssend.at[xp(d)], sbuf.at[x], ss.at[d - 1], sr.at[d - 1], at(x_=xp(d))) for d in range(1, NX)]
    for s in sx + ox:
        s.start()
    w_step(1)
    for s in sx + ox:
        s.wait_recv()
    stats = [ssend[x]] + [sbuf[xp(d)] for d in range(1, NX)]
    parts = [osend[x]] + [obuf[xp(d)] for d in range(1, NX)]
    top = functools.reduce(jnp.maximum, [s[0:1] for s in stats])
    weight = [jnp.exp2(s[0:1] - top) for s in stats]
    total = sum(s[1:2] * w for s, w in zip(stats, weight))
    att = 0.0
    for o, w in zip(parts, weight):
        att += o.astype(jnp.float32) * jnp.transpose(jnp.broadcast_to(w / total, (HD, R)))
    for h in range(H):
        ab[g, :, h * HD:(h + 1) * HD] = att[h * T:(h + 1) * T].astype(jnp.bfloat16)

    ax = [send(ab.at[g], ab.at[g], as_.at[d - 1], ar.at[d - 1], at(g_=gp(d))) for d in range(1, G)]
    for s in ax:
        s.start()
    for step in (2, 3, 4):
        w_step(step)
    for i in range(NY):
        w_over(yp(i), i).wait_recv()
    for s in ax:
        s.wait_recv()

    for a in range(2):
        total_out = 0.0
        for gg in range(G):
            wmat = wb[:, :, gg, a].reshape(NY * 2 * 32, H * HD)
            total_out += dot_nt(ab[gg], wmat)
        out_ref[:, a * 512:(a + 1) * 512] = total_out.astype(jnp.bfloat16)

    @pl.when(zh == 0)
    def _():
        zsend.wait_send()

    @pl.when(zh == 1)
    def _():
        for s in fsend:
            s.wait_send()
        far_half.wait_send()

    for s in ysend + qsend + [near_half] + wsend[1:] + ox + sx + ax:
        s.wait_send()

    @pl.when(dest_g != g)
    def _():
        wsend[0].wait_send()

    for sign, step, p in all_ring:
        ring(sign, step, p).wait_send()
    for i in range(NY):
        w_over(yp(i), i).wait_send()


def body(queries, keys, values, lengths, out_weight):
    steps = np.arange(HD // 2) * (2.0 / HD)
    inverse = (500000.0 ** -steps).astype(np.float32)
    inverse = jnp.asarray(np.concatenate([inverse, inverse])[None, :])
    vmem = pl.BlockSpec(memory_space=pltpu.VMEM)
    dma = pltpu.SemaphoreType.DMA
    bf, f32 = jnp.bfloat16, jnp.float32
    return pl.pallas_call(
        kernel,
        out_shape=(jax.ShapeDtypeStruct((T, 1024), bf), jax.ShapeDtypeStruct((T, HD), bf)),
        in_specs=[vmem] * 6,
        out_specs=(vmem, vmem),
        scratch_shapes=[
            pltpu.VMEM((2, 2, NY, 2, T, HD), bf),
            pltpu.VMEM((NX, R, HD), bf),
            pltpu.VMEM((NX, R, HD), f32),
            pltpu.VMEM((NX, R, HD), f32),
            pltpu.VMEM((NX, R, HD), f32),
            pltpu.VMEM((NX, R, HD), bf),
            pltpu.VMEM((NX, 8, R), f32),
            pltpu.VMEM((NX, R, HD), bf),
            pltpu.VMEM((NX, 8, R), f32),
            pltpu.VMEM((G, T, H * HD), bf),
            pltpu.VMEM((NY, 2, G, 2, 32, H * HD), bf),
            pltpu.VMEM((NX, R, HD), f32),
            dma((NY - 1,)), dma((NY - 1,)),
            dma, dma,
            dma((NY - 1,)), dma((NY - 1,)),
            dma((2,)), dma((2,)),
            dma((NX - 1,)), dma((NX - 1,)),
            dma((NX - 1,)), dma((NX - 1,)),
            dma((NX - 1,)), dma((NX - 1,)),
            dma((G - 1,)), dma((G - 1,)),
            dma((8,)), dma((2, G)),
            dma((2, 4, 2)), dma((2, 4, 2)),
            dma((NY,)), dma((NY,)),
            dma,
        ],
        compiler_params=pltpu.CompilerParams(
            collective_id=0, has_side_effects=True, vmem_limit_bytes=56 * 2**20
        ),
    )(queries, keys, values, lengths.reshape(1, 64), out_weight, inverse)


def solution(mesh):
    return jax.shard_map(
        body,
        mesh=mesh,
        in_specs=(P("blk", "kv"), P("blk", "kv"), P("blk", "kv"), P(), P("blk", "kv")),
        out_specs=(P("blk", "kv"), P("blk", "kv")),
        check_vma=False,
    )
```

time: 454 us -> 60.7 us (0.13)
  the two profiles are of different devices: /device:TPU:6 before, /device:TPU:257 now
where the time goes in v1:
time: 60.7 us; the launch traced here: 60.5 us
  Pallas kernels  57.6 us (95%)
  local copies, waits for them, and re-layouts  2.21 us (4%)
  between operations  0.65 us (1%)
    pallas_call x1, Pallas kernels, body(): pl.pallas_call(kernel, out_shape=(jax.ShapeDtypeStruct((T, 1024), bf), ja...  57.6 us
    unnamed x4, local copies, waits for them, and re-layouts  2.21 us

profile of v1, /device:TPU:257, one launch (start us, length us, event | category | flops | bytes accessed | tf_op | source)
XLA Modules:
  0.0 60.5 jit_solution(13288671587801706986)
XLA Ops:
  0.6 57.6 %shard_map.77 = (bf16[80,1024]{1,0:T(8,128)(2,1)}, bf16[80,128]{1,0:T(8,128)(2,1)}) custom-call(bf16[80,512]{1,0:T(8,128)(2,1)} %q_ref.1, bf16[80,128]{1,0:T(8,128)(2,1)} %k_ref.1, bf16[80,128]{1,0:T(8,128)(2,1)} %v_ref.1, s32[1,64]{1,0:T(1,128)} %bitcast.1, bf16[32,512]{1,0:T(8,128)(2,1)} %w_ref.1, f32[1,128]{1,0:T(1,128)} %constant.2.clone.inv_ref), custom_call_target="tpu_custom_call" | custom-call | tf_op jit(solution)/shard_map/pallas_call | solution.py:341
  58.3 0.0 copy-start
  58.3 1.6 %copy.10 = bf16[80,1024]{1,0:T(8,128)(2,1)} copy(bf16[80,1024]{1,0:T(8,128)(2,1)} %get-tuple-element.4) | data formatting | bytes 327680
  59.9 0.0 copy-done
  59.9 0.6 %copy.11 = bf16[80,128]{1,0:T(8,128)(2,1)} copy(bf16[80,128]{1,0:T(8,128)(2,1)S(1)} %copy-done) | data formatting | bytes 40960
Async XLA Ops:
  58.3 1.6 %copy-start = (bf16[80,128]{1,0:T(8,128)(2,1)S(1)}, bf16[80,128]{1,0:T(8,128)(2,1)}, u32[]{:S(2)}) copy-start(bf16[80,128]{1,0:T(8,128)(2,1)} %get-tuple-element.5) | copy-start | bytes 61444

commit v2 on v1

--- a/solution.py
+++ b/solution.py
@@ -17,6 +17,7 @@
 LONG_TOKENS = 8192
 TOKENS = 10240
 NEG = -1e30
+PLAN = ("WF", "", "RX", "a", "1", "", "2", "b3", "4E")
 SCALE = float(np.log2(np.e) / np.sqrt(HD))
 
 
@@ -26,8 +27,8 @@
 
 def kernel(
     q_ref, k_ref, v_ref, len_ref, w_ref, inv_ref, out_ref, cache_ref,
-    kv, qb, acc, mx, sm, osend, ssend, obuf, sbuf, ab, wb, col,
-    ys, yr, zs, zr, fs, fr, cs, cr, qs, qr, os_, or_, ss, sr, as_, ar, wds, wdr, wrs, wrr, wcs, wcr, lsem,
+    kv, qb, acc, mx, sm, osend, ssend, obuf, sbuf, ab, wa, wb, col,
+    ys, yr, zs, zr, fs, fr, cs, cr, qs, qr, os_, or_, ss, sr, as_, ar, wds, wdr, wxs, wxr, wys, wyr, wbs, wbr, wrs, wrr, wcs, wcr, wes, wer, lsem,
 ):
     blk, g = lax.axis_index("blk"), lax.axis_index("kv")
     c = lax.rem(blk, 2)
@@ -68,15 +69,11 @@
     for d in range(1, G):
         hello(at(g_=gp(d)))
     src_zh, src_x = lax.div(g, 2), 2 * lax.rem(g, 2)
-    is_src = (src_zh == zh) & (lax.div(x, 2) == lax.rem(g, 2))
+    own_w = (x == g) & (dest_g == g)
     for a in range(2):
-        for d in range(G):
-            if d == 0:
-                @pl.when(jnp.logical_not(is_src & (half == a)))
-                def _(a=a):
-                    hello(at(zh_=src_zh, x_=src_x + a))
-            else:
-                hello(at(zh_=src_zh, x_=src_x + a, g_=gp(d)))
+        @pl.when(jnp.logical_not(own_w & (half == a)))
+        def _(a=a):
+            hello(at(zh_=src_zh, x_=src_x + a, g_=x))
 
     lens = jnp.broadcast_to(len_ref[...].astype(jnp.float32), (8, 64))
     tri = (lax.broadcasted_iota(jnp.int32, (64, 64), 0) < lax.broadcasted_iota(jnp.int32, (64, 64), 1))
@@ -104,7 +101,7 @@
     for h in range(H):
         qb[x, h * T:(h + 1) * T, :] = rotate(q_ref[:, h * HD:(h + 1) * HD])
 
-    pl.semaphore_wait(bar, 2 + (NY - 1) + (NX - 1) + (G - 1) + 7 + jnp.where(dest_g == g, 0, 1))
+    pl.semaphore_wait(bar, 2 + (NY - 1) + (NX - 1) + (G - 1) + 2 - jnp.where(own_w, 1, 0))
 
     mine = kv.at[zh, c, y]
     zsend = send(mine, mine, zs, zr, at(zh_=1 - zh))
@@ -113,30 +110,42 @@
     def _():
         zsend.start()
 
-    ysend = [send(mine, mine, ys.at[d - 1], yr.at[d - 1], at(y_=yp(d))) for d in range(1, NY)]
+    def tree(zk, ss_, rs_):
+        me = kv.at[zk, c, y]
+        first = [send(me, me, ss_.at[i], rs_.at[i], at(y_=yp(d))) for i, d in enumerate((2, -2, 1, -1))]
+        second = []
+        for i, sign in enumerate((1, -1)):
+            whole = kv.at[zk, c, yp(-2 * sign)]
+            part = kv.at[zk, c, yp(-2 * sign), i]
+            second.append(send(whole, whole, ss_.at[4 + i], rs_.at[4 + i], at(y_=yp(sign))))
+            second.append(send(part, part, ss_.at[6 + i], rs_.at[6 + i], at(y_=yp(2 * sign))))
+        return first, second
+
+    near1, near2 = tree(zh, ys, yr)
+    far1, far2 = tree(0, fs, fr)
     qsend = [send(qb.at[x], qb.at[x], qs.at[d - 1], qr.at[d - 1], at(x_=xp(d))) for d in range(1, NX)]
-    for d in (4, 3, 5, 2, 6, 1, 7):
-        ysend[d - 1].start()
-    for s in qsend:
+    for s in near1 + qsend:
         s.start()
-    slot = wb.at[y, c, g, half]
-    wsend = []
-    for dz in range(2):
-        for dx in range(NX):
-            i = dz * NX + dx
-            s = send(w_ref, slot, wds.at[i], wdr.at[half, g], at(zh_=lax.rem(zh + dz, 2), x_=xp(dx), g_=dest_g))
-            if i:
-                s.start()
-            else:
-                @pl.when(dest_g != g)
-                def _(s=s):
-                    s.start()
-            wsend.append(s)
-    own_w = pltpu.make_async_copy(w_ref, slot, lsem)
-
-    @pl.when(dest_g == g)
-    def _():
-        own_w.start()
+
+    def first_hop(a, dz):
+        slot = wa.at[y, c, g] if a == 0 else wb.at[g, y, c]
+        return send(w_ref, slot, wds.at[dz], wdr.at[a], at(zh_=lax.rem(zh + dz, 2), x_=g, g_=dest_g))
+
+    def own_copy(a):
+        return pltpu.make_async_copy(w_ref, wa.at[y, c, g] if a == 0 else wb.at[g, y, c], lsem)
+
+    for a in range(2):
+        @pl.when(half == a)
+        def _(a=a):
+            first_hop(a, 1).start()
+
+            @pl.when(own_w)
+            def _():
+                own_copy(a).start()
+
+            @pl.when(jnp.logical_not(own_w))
+            def _():
+                first_hop(a, 0).start()
 
     for i in range(NX):
         tk = (row + ((zh * NX + i) * 16 + 2 * y + c) * T).astype(jnp.float32)
@@ -148,14 +157,75 @@
     sm[...] = jnp.zeros(sm.shape, jnp.float32)
     acc[...] = jnp.zeros(acc.shape, jnp.float32)
 
-    other = kv.at[0, c, y]
-    fsend = [send(other, other, fs.at[d - 1], fr.at[d - 1], at(y_=yp(d))) for d in range(1, NY)]
+    def second(first, then):
+        for s in first[:2]:
+            s.wait_recv()
+        for s in then:
+            s.start()
+
+    second(near1, near2)
 
     @pl.when(zh == 1)
     def _():
         zsend.wait_recv()
+        for s in far1:
+            s.start()
+
+    def far_second():
+        @pl.when(zh == 1)
+        def _():
+            second(far1, far2)
+
+    wy = [send(wb.at[x, y, c], wb.at[x, y, c], wys.at[d - 1], wyr.at[d - 1], at(y_=yp(d))) for d in range(1, NY)]
+    wx = [send(wa.at[y, c, x], wa.at[y, c, x], wxs.at[d - 1], wxr.at[d - 1], at(x_=xp(d))) for d in range(1, NX)]
+
+    def cross_part(i, k):
+        return wb.at[i, pl.ds(4 * k, 4), c]
+
+    def cross(d, k):
+        part = cross_part(x, k)
+        return send(part, part, wbs.at[d - 1, k], wbr.at[d - 1, k], at(x_=xp(d)))
+
+    def ring(sign, step, p):
+        i = 0 if sign > 0 else 1
+        piece = wa.at[yp(-sign * (step - 1)), c, pl.ds(2 * p, 2)]
+        return send(piece, piece, wrs.at[i, step - 1, p], wrr.at[i, step - 1, p], at(y_=yp(sign)))
+
+    def ring_pieces(sign, step):
+        return (0, 1) if step < 4 else ((0,) if sign > 0 else (1,))
+
+    def w_over(yy, i):
+        return send(wa.at[yy, c], wa.at[yy, c], wcs.at[i], wcr.at[i], at(c_=1 - c))
+
+    def wb_over(d):
+        part = wb.at[xp(d), :, c]
+        return send(part, part, wes.at[d], wer.at[d], at(c_=1 - c))
+
+    all_ring = [(sign, step, p) for step in range(1, 5) for sign in (1, -1) for p in ring_pieces(sign, step)]
+
+    def w_first():
+        for a in range(2):
+            here = own_w & (half == a)
+
+            @pl.when(here)
+            def _(a=a):
+                own_copy(a).wait()
+
+            @pl.when(jnp.logical_not(here))
+            def _(a=a):
+                first_hop(a, 0).wait_recv()
+        for s in wx:
+            s.start()
         for d in (4, 3, 5, 2, 6, 1, 7):
-            fsend[d - 1].start()
+            wy[d - 1].start()
+
+    def w_ring_begin():
+        for s in wx:
+            s.wait_recv()
+        for p in range(2):
+            for sign in (1, -1):
+                ring(sign, 1, p).start()
+        w_over(y, 0).start()
 
     def chunk(zk, ck):
         sk = zk * NX + x
@@ -201,44 +271,20 @@
     def over(zk, i):
         return send(kv.at[zk, c], kv.at[zk, c], cs.at[i], cr.at[i], at(c_=1 - c))
 
-    near_half = over(zh, 0)
-    far_half = over(0, 1)
-    for s in ysend:
-        s.wait_recv()
-    near_half.start()
-    for s in qsend:
-        s.wait_recv()
-    chunk(zh, c)
-
-    def ring(sign, step, p):
-        i = 0 if sign > 0 else 1
-        piece = wb.at[yp(-sign * (step - 1)), c, pl.ds(2 * p, 2)]
-        return send(piece, piece, wrs.at[i, step - 1, p], wrr.at[i, step - 1, p], at(y_=yp(sign)))
-
-    def ring_pieces(sign, step):
-        return (0, 1) if step < 4 else ((0,) if sign > 0 else (1,))
-
-    def w_over(yy, i):
-        return send(wb.at[yy, c], wb.at[yy, c], wcs.at[i], wcr.at[i], at(c_=1 - c))
-
-    all_ring = [(sign, step, p) for step in range(1, 5) for sign in (1, -1) for p in ring_pieces(sign, step)]
-
-    def w_begin():
-        for a in range(2):
-            for gg in range(G):
-                is_own = (gg == g) & (dest_g == g) & (half == a)
-
-                @pl.when(is_own)
-                def _():
-                    own_w.wait()
-
-                @pl.when(jnp.logical_not(is_own))
-                def _(a=a, gg=gg):
-                    send(w_ref, wb.at[y, c, gg, a], wds.at[0], wdr.at[a, gg], at(c_=1 - c)).wait_recv()
-        for p in range(2):
-            for sign in (1, -1):
-                ring(sign, 1, p).start()
-        w_over(y, 0).start()
+    def w_cross():
+        for s in wy:
+            s.wait_recv()
+        wb_over(0).start()
+
+    def w_cross_go(k):
+        for d in (2, 1, 3):
+            cross(d, k).start()
+
+    def w_cross_end():
+        for d in range(1, NX):
+            for k in range(2):
+                cross(d, k).wait_recv()
+            wb_over(NX - d).start()
 
     def w_step(step):
         for p in range(2):
@@ -251,18 +297,61 @@
         if step < 4:
             w_over(yp(-step), 8 - step).start()
 
-    w_begin()
-    near_half.wait_recv()
-    chunk(zh, 1 - c)
-
-    @pl.when(zh == 1)
-    def _():
-        for s in fsend:
-            s.wait_recv()
-        far_half.start()
-        chunk(0, c)
-        far_half.wait_recv()
-        chunk(0, 1 - c)
+    work = {
+        "W": w_first, "R": w_ring_begin, "X": w_cross, "E": w_cross_end,
+        "a": lambda: w_cross_go(0), "b": lambda: w_cross_go(1), "F": far_second,
+    }
+    for step in range(1, 5):
+        work[str(step)] = functools.partial(w_step, step)
+
+    def turn(i):
+        for name in PLAN[i]:
+            work[name]()
+
+    near_half = over(zh, 0)
+    far_half = over(0, 1)
+    turn(0)
+    for s in near1[2:] + near2:
+        s.wait_recv()
+    near_half.start()
+    for s in qsend:
+        s.wait_recv()
+    turn(1)
+
+    def stage(i, _):
+        @pl.when(i == 1)
+        def _():
+            turn(2)
+            near_half.wait_recv()
+
+        @pl.when(i == 2)
+        def _():
+            turn(3)
+
+            @pl.when(zh == 1)
+            def _():
+                for s in far1[2:] + far2:
+                    s.wait_recv()
+                far_half.start()
+
+            turn(4)
+
+        @pl.when(i == 3)
+        def _():
+            turn(5)
+
+            @pl.when(zh == 1)
+            def _():
+                far_half.wait_recv()
+
+        @pl.when((i < 2) | (zh == 1))
+        def _():
+            chunk(jnp.where(i < 2, zh, 0), jnp.where(lax.rem(i, 2) == 0, c, 1 - c))
+
+        return 0
+
+    lax.fori_loop(0, 4, stage, 0)
+    turn(6)
 
     lane_r = lax.broadcasted_iota(jnp.int32, (R, HD), 1)
 
@@ -277,7 +366,7 @@
     sx = [send(ssend.at[xp(d)], sbuf.at[x], ss.at[d - 1], sr.at[d - 1], at(x_=xp(d))) for d in range(1, NX)]
     for s in sx + ox:
         s.start()
-    w_step(1)
+    turn(7)
     for s in sx + ox:
         s.wait_recv()
     stats = [ssend[x]] + [sbuf[xp(d)] for d in range(1, NX)]
@@ -294,17 +383,18 @@
     ax = [send(ab.at[g], ab.at[g], as_.at[d - 1], ar.at[d - 1], at(g_=gp(d))) for d in range(1, G)]
     for s in ax:
         s.start()
-    for step in (2, 3, 4):
-        w_step(step)
+    turn(8)
     for i in range(NY):
         w_over(yp(i), i).wait_recv()
+    for d in range(NX):
+        wb_over(d).wait_recv()
     for s in ax:
         s.wait_recv()
 
     for a in range(2):
         total_out = 0.0
         for gg in range(G):
-            wmat = wb[:, :, gg, a].reshape(NY * 2 * 32, H * HD)
+            wmat = (wa[:, :, gg] if a == 0 else wb[gg]).reshape(NY * 2 * 32, H * HD)
             total_out += dot_nt(ab[gg], wmat)
         out_ref[:, a * 512:(a + 1) * 512] = total_out.astype(jnp.bfloat16)
 
@@ -314,21 +404,24 @@
 
     @pl.when(zh == 1)
     def _():
-        for s in fsend:
+        for s in far1 + far2:
             s.wait_send()
         far_half.wait_send()
 
-    for s in ysend + qsend + [near_half] + wsend[1:] + ox + sx + ax:
+    for s in near1 + near2 + qsend + [near_half] + wx + wy + [cross(d, k) for d in range(1, NX) for k in range(2)] + ox + sx + ax:
         s.wait_send()
-
-    @pl.when(dest_g != g)
+    first_hop(0, 1).wait_send()
+
+    @pl.when(jnp.logical_not(own_w))
     def _():
-        wsend[0].wait_send()
+        first_hop(0, 0).wait_send()
 
     for sign, step, p in all_ring:
         ring(sign, step, p).wait_send()
     for i in range(NY):
         w_over(yp(i), i).wait_send()
+    for d in range(NX):
+        wb_over(d).wait_send()
 
 
 def body(queries, keys, values, lengths, out_weight):
@@ -354,19 +447,24 @@
             pltpu.VMEM((NX, R, HD), bf),
             pltpu.VMEM((NX, 8, R), f32),
             pltpu.VMEM((G, T, H * HD), bf),
-            pltpu.VMEM((NY, 2, G, 2, 32, H * HD), bf),
+            pltpu.VMEM((NY, 2, G, 32, H * HD), bf),
+            pltpu.VMEM((G, NY, 2, 32, H * HD), bf),
             pltpu.VMEM((NX, R, HD), f32),
-            dma((NY - 1,)), dma((NY - 1,)),
+            dma((8,)), dma((8,)),
             dma, dma,
-            dma((NY - 1,)), dma((NY - 1,)),
+            dma((8,)), dma((8,)),
             dma((2,)), dma((2,)),
             dma((NX - 1,)), dma((NX - 1,)),
             dma((NX - 1,)), dma((NX - 1,)),
             dma((NX - 1,)), dma((NX - 1,)),
             dma((G - 1,)), dma((G - 1,)),
-            dma((8,)), dma((2, G)),
+            dma((2,)), dma((2,)),
+            dma((NX - 1,)), dma((NX - 1,)),
+            dma((NY - 1,)), dma((NY - 1,)),
+            dma((NX - 1, 2)), dma((NX - 1, 2)),
             dma((2, 4, 2)), dma((2, 4, 2)),
             dma((NY,)), dma((NY,)),
+            dma((NX,)), dma((NX,)),
             dma,
         ],
         compiler_params=pltpu.CompilerParams(

time: 60.7 us -> 56.3 us (0.928)
  the two profiles are of different devices: /device:TPU:257 before, /device:TPU:6 now
where the time goes in v2:
time: 56.3 us; the launch traced here: 56.1 us
  Pallas kernels  53.3 us (95%)
  local copies, waits for them, and re-layouts  2.21 us (4%)
  between operations  0.65 us (1%)
    pallas_call x1, Pallas kernels, body(): pl.pallas_call(kernel, out_shape=(jax.ShapeDtypeStruct((T, 1024), bf), ja...  53.3 us
    unnamed x4, local copies, waits for them, and re-layouts  2.21 us

profile of v2, /device:TPU:6, one launch (start us, length us, event | category | flops | bytes accessed | tf_op | source)
XLA Modules:
  0.0 56.1 jit_solution(6475228655395524913)
XLA Ops:
  0.6 53.3 %shard_map.77 = (bf16[80,1024]{1,0:T(8,128)(2,1)}, bf16[80,128]{1,0:T(8,128)(2,1)}) custom-call(bf16[80,512]{1,0:T(8,128)(2,1)} %q_ref.1, bf16[80,128]{1,0:T(8,128)(2,1)} %k_ref.1, bf16[80,128]{1,0:T(8,128)(2,1)} %v_ref.1, s32[1,64]{1,0:T(1,128)} %bitcast.1, bf16[32,512]{1,0:T(8,128)(2,1)} %w_ref.1, f32[1,128]{1,0:T(1,128)} %constant.2.clone.inv_ref), custom_call_target="tpu_custom_call" | custom-call | tf_op jit(solution)/shard_map/pallas_call | solution.py:434
  53.9 0.0 copy-start
  53.9 1.6 %copy.10 = bf16[80,1024]{1,0:T(8,128)(2,1)} copy(bf16[80,1024]{1,0:T(8,128)(2,1)} %get-tuple-element.4) | data formatting | bytes 327680
  55.5 0.0 copy-done
  55.5 0.6 %copy.11 = bf16[80,128]{1,0:T(8,128)(2,1)} copy(bf16[80,128]{1,0:T(8,128)(2,1)S(1)} %copy-done) | data formatting | bytes 40960
Async XLA Ops:
  53.9 1.6 %copy-start = (bf16[80,128]{1,0:T(8,128)(2,1)S(1)}, bf16[80,128]{1,0:T(8,128)(2,1)}, u32[]{:S(2)}) copy-start(bf16[80,128]{1,0:T(8,128)(2,1)} %get-tuple-element.5) | copy-start | bytes 61444

commit v3 on v2

--- a/solution.py
+++ b/solution.py
@@ -17,7 +17,7 @@
 LONG_TOKENS = 8192
 TOKENS = 10240
 NEG = -1e30
-PLAN = ("WF", "", "RX", "a", "1", "", "2", "b3", "4E")
+PLAN = ("WF", "", "RXa", "", "1", "", "2", "b3", "E4")
 SCALE = float(np.log2(np.e) / np.sqrt(HD))
 
 
@@ -179,12 +179,12 @@
     wy = [send(wb.at[x, y, c], wb.at[x, y, c], wys.at[d - 1], wyr.at[d - 1], at(y_=yp(d))) for d in range(1, NY)]
     wx = [send(wa.at[y, c, x], wa.at[y, c, x], wxs.at[d - 1], wxr.at[d - 1], at(x_=xp(d))) for d in range(1, NX)]
 
-    def cross_part(i, k):
-        return wb.at[i, pl.ds(4 * k, 4), c]
-
-    def cross(d, k):
-        part = cross_part(x, k)
-        return send(part, part, wbs.at[d - 1, k], wbr.at[d - 1, k], at(x_=xp(d)))
+    whole_x = wb.at[x, :, c]
+    cross1 = [send(whole_x, whole_x, wbs.at[i], wbr.at[i], at(x_=xp(d))) for i, d in enumerate((1, NX - 1))]
+    cross2 = []
+    for i, d in enumerate((1, NX - 1)):
+        part = wb.at[xp(NX - d), pl.ds(4 * i, 4), c]
+        cross2.append(send(part, part, wbs.at[2 + i], wbr.at[2 + i], at(x_=xp(d))))
 
     def ring(sign, step, p):
         i = 0 if sign > 0 else 1
@@ -276,15 +276,22 @@
             s.wait_recv()
         wb_over(0).start()
 
-    def w_cross_go(k):
-        for d in (2, 1, 3):
-            cross(d, k).start()
+    def w_cross_one():
+        for s in cross1:
+            s.start()
+
+    def w_cross_two():
+        for s in cross1:
+            s.wait_recv()
+        for s in cross2:
+            s.start()
+        wb_over(1).start()
+        wb_over(NX - 1).start()
 
     def w_cross_end():
-        for d in range(1, NX):
-            for k in range(2):
-                cross(d, k).wait_recv()
-            wb_over(NX - d).start()
+        for s in cross2:
+            s.wait_recv()
+        wb_over(2).start()
 
     def w_step(step):
         for p in range(2):
@@ -299,7 +306,7 @@
 
     work = {
         "W": w_first, "R": w_ring_begin, "X": w_cross, "E": w_cross_end,
-        "a": lambda: w_cross_go(0), "b": lambda: w_cross_go(1), "F": far_second,
+        "a": w_cross_one, "b": w_cross_two, "F": far_second,
     }
     for step in range(1, 5):
         work[str(step)] = functools.partial(w_step, step)
@@ -355,17 +362,17 @@
 
     lane_r = lax.broadcasted_iota(jnp.int32, (R, HD), 1)
 
-    def pack(d, _):
-        i = lax.rem(x + d, NX)
+    def pack(i):
         osend[i] = acc[i].astype(jnp.bfloat16)
         ssend[i] = jnp.transpose(jnp.where(lane_r == 0, mx[i], sm[i]))[:8]
-        return 0
-
-    lax.fori_loop(0, NX, pack, 0)
+
     ox = [send(osend.at[xp(d)], obuf.at[x], os_.at[d - 1], or_.at[d - 1], at(x_=xp(d))) for d in range(1, NX)]
     sx = [send(ssend.at[xp(d)], sbuf.at[x], ss.at[d - 1], sr.at[d - 1], at(x_=xp(d))) for d in range(1, NX)]
-    for s in sx + ox:
-        s.start()
+    for d in (2, 1, 3, 0):
+        pack(xp(d))
+        if d:
+            ox[d - 1].start()
+            sx[d - 1].start()
     turn(7)
     for s in sx + ox:
         s.wait_recv()
@@ -388,15 +395,17 @@
         w_over(yp(i), i).wait_recv()
     for d in range(NX):
         wb_over(d).wait_recv()
-    for s in ax:
-        s.wait_recv()
-
+
+    total_out = [0.0, 0.0]
+    for d in range(G):
+        gg = gp(d)
+        if d:
+            ax[G - d - 1].wait_recv()
+        for a in range(2):
+            wmat = (wa[:, :, gg] if a == 0 else wb[gg]).reshape(NY * 2 * 32, H * HD)
+            total_out[a] += dot_nt(ab[gg], wmat)
     for a in range(2):
-        total_out = 0.0
-        for gg in range(G):
-            wmat = (wa[:, :, gg] if a == 0 else wb[gg]).reshape(NY * 2 * 32, H * HD)
-            total_out += dot_nt(ab[gg], wmat)
-        out_ref[:, a * 512:(a + 1) * 512] = total_out.astype(jnp.bfloat16)
+        out_ref[:, a * 512:(a + 1) * 512] = total_out[a].astype(jnp.bfloat16)
 
     @pl.when(zh == 0)
     def _():
@@ -408,7 +417,7 @@
             s.wait_send()
         far_half.wait_send()
 
-    for s in near1 + near2 + qsend + [near_half] + wx + wy + [cross(d, k) for d in range(1, NX) for k in range(2)] + ox + sx + ax:
+    for s in near1 + near2 + qsend + [near_half] + wx + wy + cross1 + cross2 + ox + sx + ax:
         s.wait_send()
     first_hop(0, 1).wait_send()
 
@@ -461,7 +470,7 @@
             dma((2,)), dma((2,)),
             dma((NX - 1,)), dma((NX - 1,)),
             dma((NY - 1,)), dma((NY - 1,)),
-            dma((NX - 1, 2)), dma((NX - 1, 2)),
+            dma((4,)), dma((4,)),
             dma((2, 4, 2)), dma((2, 4, 2)),
             dma((NY,)), dma((NY,)),
             dma((NX,)), dma((NX,)),

time: 56.3 us -> 54.4 us (0.966); the launches traced: 56.1 us -> 53.5 us
  Pallas kernels: 53.3 us -> 50.7 us
    pallas_call x1, Pallas kernels: 53.3 us -> 50.7 us  [body(): pl.pallas_call(kernel, out_shape=(jax.ShapeDtypeStruct((T, 1024), bf), ja...]
where the time goes in v3:
time: 54.4 us; the launch traced here: 53.5 us
  Pallas kernels  50.7 us (93%)
  local copies, waits for them, and re-layouts  2.21 us (4%)
  between operations  0.65 us (1%)
    pallas_call x1, Pallas kernels, body(): pl.pallas_call(kernel, out_shape=(jax.ShapeDtypeStruct((T, 1024), bf), ja...  50.7 us
    unnamed x4, local copies, waits for them, and re-layouts  2.21 us

profile of v3, /device:TPU:6, one launch (start us, length us, event | category | flops | bytes accessed | tf_op | source)
XLA Modules:
  0.0 53.5 jit_solution(4152883263632827794)
XLA Ops:
  0.6 50.7 %shard_map.77 = (bf16[80,1024]{1,0:T(8,128)(2,1)}, bf16[80,128]{1,0:T(8,128)(2,1)}) custom-call(bf16[80,512]{1,0:T(8,128)(2,1)} %q_ref.1, bf16[80,128]{1,0:T(8,128)(2,1)} %k_ref.1, bf16[80,128]{1,0:T(8,128)(2,1)} %v_ref.1, s32[1,64]{1,0:T(1,128)} %bitcast.1, bf16[32,512]{1,0:T(8,128)(2,1)} %w_ref.1, f32[1,128]{1,0:T(1,128)} %constant.2.clone.inv_ref), custom_call_target="tpu_custom_call" | custom-call | tf_op jit(solution)/shard_map/pallas_call | solution.py:443
  51.3 0.0 copy-start
  51.3 1.6 %copy.10 = bf16[80,1024]{1,0:T(8,128)(2,1)} copy(bf16[80,1024]{1,0:T(8,128)(2,1)} %get-tuple-element.4) | data formatting | bytes 327680
  52.9 0.0 copy-done
  52.9 0.6 %copy.11 = bf16[80,128]{1,0:T(8,128)(2,1)} copy(bf16[80,128]{1,0:T(8,128)(2,1)S(1)} %copy-done) | data formatting | bytes 40960
Async XLA Ops:
  51.3 1.6 %copy-start = (bf16[80,128]{1,0:T(8,128)(2,1)S(1)}, bf16[80,128]{1,0:T(8,128)(2,1)}, u32[]{:S(2)}) copy-start(bf16[80,128]{1,0:T(8,128)(2,1)} %get-tuple-element.5) | copy-start | bytes 61444

commit v4 on v3

--- a/solution.py
+++ b/solution.py
@@ -17,7 +17,7 @@
 LONG_TOKENS = 8192
 TOKENS = 10240
 NEG = -1e30
-PLAN = ("WF", "", "RXa", "", "1", "", "2", "b3", "E4")
+PLAN = ("WFT", "R", "Xa", "", "1", "", "2", "b3", "E4")
 SCALE = float(np.log2(np.e) / np.sqrt(HD))
 
 
@@ -176,7 +176,14 @@
         def _():
             second(far1, far2)
 
-    wy = [send(wb.at[x, y, c], wb.at[x, y, c], wys.at[d - 1], wyr.at[d - 1], at(y_=yp(d))) for d in range(1, NY)]
+    whole_y = wb.at[x, y, c]
+    wy1 = [send(whole_y, whole_y, wys.at[i], wyr.at[i], at(y_=yp(d))) for i, d in enumerate((2, -2, 1, -1))]
+    wy2 = []
+    for i, sign in enumerate((1, -1)):
+        full = wb.at[x, yp(-2 * sign), c]
+        part = wb.at[x, yp(-2 * sign), c, pl.ds(16 * i, 16)]
+        wy2.append(send(full, full, wys.at[4 + i], wyr.at[4 + i], at(y_=yp(sign))))
+        wy2.append(send(part, part, wys.at[6 + i], wyr.at[6 + i], at(y_=yp(2 * sign))))
     wx = [send(wa.at[y, c, x], wa.at[y, c, x], wxs.at[d - 1], wxr.at[d - 1], at(x_=xp(d))) for d in range(1, NX)]
 
     whole_x = wb.at[x, :, c]
@@ -216,8 +223,8 @@
                 first_hop(a, 0).wait_recv()
         for s in wx:
             s.start()
-        for d in (4, 3, 5, 2, 6, 1, 7):
-            wy[d - 1].start()
+        for s in wy1:
+            s.start()
 
     def w_ring_begin():
         for s in wx:
@@ -272,7 +279,7 @@
         return send(kv.at[zk, c], kv.at[zk, c], cs.at[i], cr.at[i], at(c_=1 - c))
 
     def w_cross():
-        for s in wy:
+        for s in wy1[2:] + wy2:
             s.wait_recv()
         wb_over(0).start()
 
@@ -306,7 +313,7 @@
 
     work = {
         "W": w_first, "R": w_ring_begin, "X": w_cross, "E": w_cross_end,
-        "a": w_cross_one, "b": w_cross_two, "F": far_second,
+        "a": w_cross_one, "b": w_cross_two, "F": far_second, "T": lambda: second(wy1, wy2),
     }
     for step in range(1, 5):
         work[str(step)] = functools.partial(w_step, step)
@@ -417,7 +424,7 @@
             s.wait_send()
         far_half.wait_send()
 
-    for s in near1 + near2 + qsend + [near_half] + wx + wy + cross1 + cross2 + ox + sx + ax:
+    for s in near1 + near2 + qsend + [near_half] + wx + wy1 + wy2 + cross1 + cross2 + ox + sx + ax:
         s.wait_send()
     first_hop(0, 1).wait_send()
 
@@ -469,7 +476,7 @@
             dma((G - 1,)), dma((G - 1,)),
             dma((2,)), dma((2,)),
             dma((NX - 1,)), dma((NX - 1,)),
-            dma((NY - 1,)), dma((NY - 1,)),
+            dma((8,)), dma((8,)),
             dma((4,)), dma((4,)),
             dma((2, 4, 2)), dma((2, 4, 2)),
             dma((NY,)), dma((NY,)),

time: 54.4 us -> 54.2 us (level)
  no operation moved by 1% of the time
where the time goes in v4:
time: 54.2 us; the launch traced here: 53.5 us
  Pallas kernels  50.6 us (93%)
  local copies, waits for them, and re-layouts  2.21 us (4%)
  between operations  0.65 us (1%)
    pallas_call x1, Pallas kernels, body(): pl.pallas_call(kernel, out_shape=(jax.ShapeDtypeStruct((T, 1024), bf), ja...  50.6 us
    unnamed x4, local copies, waits for them, and re-layouts  2.21 us

profile of v4, /device:TPU:6, one launch (start us, length us, event | category | flops | bytes accessed | tf_op | source)
XLA Modules:
  0.0 53.5 jit_solution(7064261664279668814)
XLA Ops:
  0.6 50.6 %shard_map.77 = (bf16[80,1024]{1,0:T(8,128)(2,1)}, bf16[80,128]{1,0:T(8,128)(2,1)}) custom-call(bf16[80,512]{1,0:T(8,128)(2,1)} %q_ref.1, bf16[80,128]{1,0:T(8,128)(2,1)} %k_ref.1, bf16[80,128]{1,0:T(8,128)(2,1)} %v_ref.1, s32[1,64]{1,0:T(1,128)} %bitcast.1, bf16[32,512]{1,0:T(8,128)(2,1)} %w_ref.1, f32[1,128]{1,0:T(1,128)} %constant.2.clone.inv_ref), custom_call_target="tpu_custom_call" | custom-call | tf_op jit(solution)/shard_map/pallas_call | solution.py:450
  51.2 0.0 copy-start
  51.2 1.6 %copy.10 = bf16[80,1024]{1,0:T(8,128)(2,1)} copy(bf16[80,1024]{1,0:T(8,128)(2,1)} %get-tuple-element.4) | data formatting | bytes 327680
  52.8 0.0 copy-done
  52.8 0.6 %copy.11 = bf16[80,128]{1,0:T(8,128)(2,1)} copy(bf16[80,128]{1,0:T(8,128)(2,1)S(1)} %copy-done) | data formatting | bytes 40960
Async XLA Ops:
  51.2 1.6 %copy-start = (bf16[80,128]{1,0:T(8,128)(2,1)S(1)}, bf16[80,128]{1,0:T(8,128)(2,1)}, u32[]{:S(2)}) copy-start(bf16[80,128]{1,0:T(8,128)(2,1)} %get-tuple-element.5) | copy-start | bytes 61444

commit v5 on v4

--- a/solution.py
+++ b/solution.py
@@ -124,8 +124,6 @@
     near1, near2 = tree(zh, ys, yr)
     far1, far2 = tree(0, fs, fr)
     qsend = [send(qb.at[x], qb.at[x], qs.at[d - 1], qr.at[d - 1], at(x_=xp(d))) for d in range(1, NX)]
-    for s in near1 + qsend:
-        s.start()
 
     def first_hop(a, dz):
         slot = wa.at[y, c, g] if a == 0 else wb.at[g, y, c]
@@ -146,6 +144,9 @@
             @pl.when(jnp.logical_not(own_w))
             def _():
                 first_hop(a, 0).start()
+
+    for s in near1 + qsend:
+        s.start()
 
     for i in range(NX):
         tk = (row + ((zh * NX + i) * 16 + 2 * y + c) * T).astype(jnp.float32)

time: 54.2 us -> 53.2 us (0.982)
  Pallas kernels: 50.6 us -> 50 us
    pallas_call x1, Pallas kernels: 50.6 us -> 50 us  [body(): pl.pallas_call(kernel, out_shape=(jax.ShapeDtypeStruct((T, 1024), bf), ja...]
where the time goes in v5:
time: 53.2 us; the launch traced here: 52.8 us
  Pallas kernels  50 us (94%)
  local copies, waits for them, and re-layouts  2.21 us (4%)
  between operations  0.65 us (1%)
    pallas_call x1, Pallas kernels, body(): pl.pallas_call(kernel, out_shape=(jax.ShapeDtypeStruct((T, 1024), bf), ja...  50 us
    unnamed x4, local copies, waits for them, and re-layouts  2.21 us

profile of v5, /device:TPU:6, one launch (start us, length us, event | category | flops | bytes accessed | tf_op | source)
XLA Modules:
  0.0 52.8 jit_solution(4610097795529098706)
XLA Ops:
  0.6 50.0 %shard_map.77 = (bf16[80,1024]{1,0:T(8,128)(2,1)}, bf16[80,128]{1,0:T(8,128)(2,1)}) custom-call(bf16[80,512]{1,0:T(8,128)(2,1)} %q_ref.1, bf16[80,128]{1,0:T(8,128)(2,1)} %k_ref.1, bf16[80,128]{1,0:T(8,128)(2,1)} %v_ref.1, s32[1,64]{1,0:T(1,128)} %bitcast.1, bf16[32,512]{1,0:T(8,128)(2,1)} %w_ref.1, f32[1,128]{1,0:T(1,128)} %constant.2.clone.inv_ref), custom_call_target="tpu_custom_call" | custom-call | tf_op jit(solution)/shard_map/pallas_call | solution.py:451
  50.6 0.0 copy-start
  50.6 1.6 %copy.10 = bf16[80,1024]{1,0:T(8,128)(2,1)} copy(bf16[80,1024]{1,0:T(8,128)(2,1)} %get-tuple-element.4) | data formatting | bytes 327680
  52.2 0.0 copy-done
  52.2 0.6 %copy.11 = bf16[80,128]{1,0:T(8,128)(2,1)} copy(bf16[80,128]{1,0:T(8,128)(2,1)S(1)} %copy-done) | data formatting | bytes 40960
Async XLA Ops:
  50.6 1.6 %copy-start = (bf16[80,128]{1,0:T(8,128)(2,1)S(1)}, bf16[80,128]{1,0:T(8,128)(2,1)}, u32[]{:S(2)}) copy-start(bf16[80,128]{1,0:T(8,128)(2,1)} %get-tuple-element.5) | copy-start | bytes 61444
